TPU v7x, 256 devices: a whole 4x4x8 slice. The times are simulated.
256 devices in a mesh: gx: 16 (over x, z_hi, core), gy: 4 (over z_lo), gz: 4 (over y).
Axes of the slice: x: 4, y: 4, z: 8 (z_hi: 2, z_lo: 4; z = z_hi * 4 + z_lo), core: 2. Of those that a mesh axis runs over, the one named last changes fastest.
Arguments:
- position: float32 [3, 16, 4, 4, 4096], P(None, 'gx', 'gy', 'gz'), may hold values from 0 to 4
- velocity: float32 [3, 16, 4, 4, 4096], P(None, 'gx', 'gy', 'gz'), may hold values from -4 to 4
- radius: float32 [16, 4, 4, 4096], P('gx', 'gy', 'gz'), may hold values from 0.5 to 1
- vertices: float32 [9, 16, 4, 4, 2048], P(None, 'gx', 'gy', 'gz'), may hold values from 0 to 4
- vertex_speed: float32 [9, 16, 4, 4, 2048], P(None, 'gx', 'gy', 'gz'), may hold values from -4 to 4
- angles: float32 [3], replicated, may hold values from 0.1 to 0.4
- ghost_blocks: int32 [16, 4, 4, 16], P('gx', 'gy', 'gz'), may hold values from 0 to 31
- tile_home: int32 [16, 4, 4, 64], P('gx', 'gy', 'gz'), may hold values from 0 to 31
- tile_other: int32 [16, 4, 4, 64], P('gx', 'gy', 'gz'), may hold values from 0 to 127
- wall_home: int32 [16, 4, 4, 32], P('gx', 'gy', 'gz'), may hold values from 0 to 31
- wall_block: int32 [16, 4, 4, 32], P('gx', 'gy', 'gz'), may hold values from 0 to 255
- mig_order: int32 [3, 16, 4, 4, 4096], P(None, 'gx', 'gy', 'gz'), may hold values from 0 to 4095, each once within a row
- mig_count: int32 [3, 16, 4, 4, 16], P(None, 'gx', 'gy', 'gz'), may hold values from 0 to 16, as said below
Outputs:
- position_out: float32 [3, 16, 4, 4, 4096], P(None, 'gx', 'gy', 'gz')
- velocity_out: float32 [3, 16, 4, 4, 4096], P(None, 'gx', 'gy', 'gz')
- radius_out: float32 [16, 4, 4, 4096], P('gx', 'gy', 'gz')
Inputs may be any that keep to these rules, and one draw needn't show every extreme that they name: Within every step and slab, mig_count of device p for peer q equals that of q for p, is 0 for p itself, and is 16 for the first two devices of the slab toward each other.
All inputs are finite; a program needn't handle non-finite values.
Results may differ from a plain program's by a relative error of at most 0.0003.
Values sent between devices are 32-bit elements; how exact they have to be, the bound alone decides.
A program may use at most 64 MiB of HBM per device.

v0:
```python
import functools

import jax
import jax.numpy as jnp
from jax import lax
from jax.experimental import pallas as pl
from jax.experimental.pallas import tpu as pltpu
from jax.sharding import PartitionSpec as P

MESH = pl.DeviceIdType.MESH
F32 = jnp.float32
BF16 = jnp.bfloat16

STEPS = 3
NBLK = 32
GHOST = 16
POOL = 128
TILES = 64
TTILES = 32
TRIBLK = 16
SLABS = 16
GROUP = 16
MC = 16

STIFFNESS = 20.0
DAMPING = 2.0
WALL_STIFF = 20.0
SOFTENING = 0.01
TIME_STEP = 0.02
GRAVITY = 1.0
AXIS_CENTRE = 2.0
AREA_FLOOR = 1.0
SPREAD_PAD = 0.25


def split3(values):
    high = values.astype(BF16)
    rest = values - high.astype(F32)
    middle = rest.astype(BF16)
    low = (rest - middle.astype(F32)).astype(BF16)
    return high, middle, low


def split2(values):
    high = values.astype(BF16)
    low = (values - high.astype(F32)).astype(BF16)
    return high, low


def rows_of(block):
    return [block[i : i + 1, :] for i in range(8)]


def kernel(
    pos_h, vel_h, rad_h, vert_h, speed_h, order_h, angles, ghost_ids, home_ids, other_ids,
    wall_ids, wall_picks, counts,
    pos_o, vel_o, rad_o,
    bodies, corners, speeds, order, own, pool_0, pool_1, pool_2, lent, tri_0, tri_1, tri_2,
    outgoing, arrived, lane_hot, block_hot,
    pair_sel, wall_sel, pair_out, wall_out,
    in_sem, ghost_send, ghost_recv, mig_send, mig_recv,
    zh_send, zh_recv, x_send, x_recv, xz_send, xz_recv, core_send, core_recv,
):
    pool, tri = (pool_0, pool_1, pool_2), (tri_0, tri_1, tri_2)
    gx = lax.axis_index("gx")
    gy = lax.axis_index("gy")
    gz = lax.axis_index("gz")
    me = gy * 4 + gz
    x_at, zh, core = gx // 4, (gx // 2) % 2, gx % 2
    twin = gx + 1 - 2 * core
    zmate = gx + 2 - 4 * zh

    loads = [
        pltpu.make_async_copy(vert_h, corners, in_sem.at[0]),
        pltpu.make_async_copy(speed_h, speeds, in_sem.at[1]),
        pltpu.make_async_copy(pos_h, bodies.at[pl.ds(0, 3)], in_sem.at[2]),
        pltpu.make_async_copy(vel_h, bodies.at[pl.ds(3, 3)], in_sem.at[3]),
        pltpu.make_async_copy(rad_h, bodies.at[6], in_sem.at[4]),
        pltpu.make_async_copy(order_h.at[:, pl.ds(0, 8), :], order, in_sem.at[5]),
    ]
    for load in loads:
        load.start()

    def peer_of(hop):
        peer = lax.rem(me + hop, GROUP)
        return peer, (gx, peer // 4, peer % 4)

    def x_mate(hop, z_of):
        index = lax.rem(x_at + hop, 4) * 4 + z_of * 2 + core
        return index

    faces = [
        (gx > 0, gx < SLABS - 1, (gx + 1, gy, gz)),
        (gx < SLABS - 1, gx > 0, (gx - 1, gy, gz)),
        (gy > 0, gy < 3, (gx, gy + 1, gz)),
        (gy < 3, gy > 0, (gx, gy - 1, gz)),
        (gz > 0, gz < 3, (gx, gy, gz + 1)),
        (gz < 3, gz > 0, (gx, gy, gz - 1)),
    ]

    barrier = pltpu.get_barrier_semaphore()

    def greet(hop, carry):
        pl.semaphore_signal(barrier, inc=1, device_id=peer_of(hop)[1], device_id_type=MESH)
        return carry

    lax.fori_loop(1, GROUP, greet, 0)
    for other in (twin, zmate, x_mate(1, zh), x_mate(2, zh), x_mate(3, zh)):
        pl.semaphore_signal(barrier, inc=1, device_id=(other, gy, gz), device_id_type=MESH)
    for _, borrower, target in faces[:2]:
        @pl.when(borrower)
        def _():
            pl.semaphore_signal(barrier, inc=1, device_id=target, device_id_type=MESH)

    def ghost_copy(step, face, target):
        return pltpu.make_async_remote_copy(
            src_ref=lent.at[step],
            dst_ref=pool[step].at[pl.ds(NBLK + GHOST * face, GHOST)],
            send_sem=ghost_send.at[step, face],
            recv_sem=ghost_recv.at[step, face],
            device_id=target,
            device_id_type=MESH,
        )

    def tri_copy(step, owner, target, send, recv):
        part = tri[step].at[pl.ds(owner * TRIBLK, TRIBLK)]
        return pltpu.make_async_remote_copy(
            src_ref=part,
            dst_ref=part,
            send_sem=send,
            recv_sem=recv,
            device_id=(target, gy, gz),
            device_id_type=MESH,
        )

    def zh_copy(step):
        return tri_copy(step, gx, zmate, zh_send.at[step], zh_recv.at[step])

    def core_copy(step, owner, slot):
        return tri_copy(step, owner, twin, core_send.at[step, slot], core_recv.at[step, slot])

    def x_copy(step, hop):
        return tri_copy(step, gx, x_mate(hop, zh), x_send.at[step, hop - 1], x_recv.at[step, hop - 1])

    def xz_copy(step, hop):
        return tri_copy(step, zmate, x_mate(hop, zh), xz_send.at[step, hop - 1], xz_recv.at[step, hop - 1])

    def mig_copy(step, hop):
        peer, target = peer_of(hop)
        return pltpu.make_async_remote_copy(
            src_ref=outgoing.at[step, peer // 8],
            dst_ref=arrived.at[step, me],
            send_sem=mig_send.at[step, hop],
            recv_sem=mig_recv.at[step, hop],
            device_id=target,
            device_id_type=MESH,
        )

    def send_ghosts(step):
        for row in range(7):
            own[:, row, :] = bodies[row]
        own[:, 7, :] = jnp.zeros((NBLK, 128), F32)
        for slot in range(GHOST):
            lent[step, slot] = own[ghost_ids[slot]]
        for face, (_, borrower, target) in enumerate(faces):
            @pl.when(borrower)
            def _():
                ghost_copy(step, face, target).start()
        pool[step][pl.ds(0, NBLK)] = own[...]

    def wait_ghosts(step):
        for face, (lender, _, target) in enumerate(faces):
            @pl.when(lender)
            def _():
                ghost_copy(step, face, target).wait_recv()

    def blade_move(step):
        angle = jnp.full((8, 128), angles[step], F32)
        cosine = jnp.cos(angle)[0:1]
        sine = jnp.sin(angle)[0:1]
        now = []
        for corner in range(3):
            along = corners[3 * corner]
            rel_y = corners[3 * corner + 1] - AXIS_CENTRE
            rel_z = corners[3 * corner + 2] - AXIS_CENTRE
            for j, value in enumerate((
                along,
                AXIS_CENTRE + cosine * rel_y - sine * rel_z,
                AXIS_CENTRE + sine * rel_y + cosine * rel_z,
            )):
                moved = value + TIME_STEP * speeds[3 * corner + j]
                corners[3 * corner + j] = moved
                now.append(moved)
        a, b, c = now[0:3], now[3:6], now[6:9]
        centre = [(a[i] + b[i] + c[i]) / 3.0 for i in range(3)]
        u = [b[i] - a[i] for i in range(3)]
        w = [c[i] - a[i] for i in range(3)]
        area = [
            u[1] * w[2] - u[2] * w[1],
            u[2] * w[0] - u[0] * w[2],
            u[0] * w[1] - u[1] * w[0],
        ]
        length = jnp.sqrt(area[0] * area[0] + area[1] * area[1] + area[2] * area[2])
        scale = 1.0 / jnp.maximum(length, AREA_FLOOR)
        normal = [area[i] * scale for i in range(3)]
        spread = SPREAD_PAD
        for corner in (a, b, c):
            for i in range(3):
                spread = spread + (corner[i] - centre[i]) ** 2 * (1.0 / 3.0)
        level = normal[0] * centre[0] + normal[1] * centre[1] + normal[2] * centre[2]
        rows = normal + centre + [1.0 / spread, level]
        for row in range(8):
            tri[step][pl.ds(gx * TRIBLK, TRIBLK), row, :] = rows[row]

    def start_tri(step):
        blade_move(step)
        zh_copy(step).start()
        core_copy(step, gx, 0).start()
        for hop in (1, 2, 3):
            x_copy(step, hop).start()

    def forward_tri(step):
        zh_copy(step).wait_recv()
        for hop in (1, 2, 3):
            xz_copy(step, hop).start()
        core_copy(step, zmate, 1).start()

    def finish_tri(step):
        for hop in (1, 2, 3):
            x_copy(step, hop).wait_recv()
            core_copy(step, x_mate(4 - hop, zh), 1 + hop).start()
        for hop in (1, 2, 3):
            xz_copy(step, hop).wait_recv()
            core_copy(step, x_mate(4 - hop, 1 - zh), 4 + hop).start()

    def wait_tri(step):
        for slot in range(8):
            core_copy(step, gx, slot).wait_recv()

    def prepare():
        lane = lax.broadcasted_iota(jnp.int32, (128, 256), 0)
        block = lax.broadcasted_iota(jnp.int32, (NBLK, 256), 0)
        place = lax.broadcasted_iota(jnp.int32, (1, 256), 1)
        for step in range(STEPS):
            ids = jnp.concatenate([order[step, 0:1, :], order[step, 1:2, :]], axis=1)
            lane_hot[step] = (jnp.bitwise_and(ids, 127) == lane).astype(F32).astype(BF16)
            limit = jnp.zeros((1, 256), jnp.int32)
            for peer in range(GROUP):
                limit = jnp.where(lax.shift_right_logical(place, 4) == peer, counts[step, peer], limit)
            filled = jnp.bitwise_and(place, 15) < limit
            hot = lax.shift_right_logical(ids, 7) == block
            block_hot[step, 0] = hot.astype(F32)
            block_hot[step, 1] = jnp.logical_and(hot, filled).astype(F32)
        home = lax.broadcasted_iota(jnp.int32, (1, 128), 1)
        for tile in range(TILES):
            pair_sel[pl.ds(tile, 1)] = (home == home_ids[tile]).astype(F32)
        for tile in range(TTILES):
            wall_sel[pl.ds(tile, 1)] = (home == wall_ids[tile]).astype(F32)

    def pair_forces(step):
        def tile_body(tile, carry):
            mine = rows_of(own[home_ids[tile]])
            px, py, pz, pu, pv, pw, pr, _ = [jnp.broadcast_to(r, (8, 128)) for r in mine]
            theirs = pool[step][other_ids[tile]].T
            force = [jnp.zeros((8, 128), F32) for _ in range(3)]
            for part in range(16):
                q = theirs[8 * part : 8 * part + 8, :]
                qx, qy, qz, qu, qv, qw, qr = [
                    jnp.broadcast_to(q[:, i : i + 1], (8, 128)) for i in range(7)
                ]
                dx, dy, dz = px - qx, py - qy, pz - qz
                square = dx * dx + dy * dy + dz * dz + SOFTENING
                speed = (pu - qu) * dx + (pv - qv) * dy + (pw - qw) * dz
                reach = pr + qr
                scaled = square * reach
                ratio = lax.rsqrt(scaled * reach)
                dist = scaled * ratio
                over = reach * ratio
                overlap = jnp.maximum(reach - dist, 0.0)
                factor = STIFFNESS - (DAMPING * speed) * over
                strength = qr * ratio * overlap * factor
                force[0] += strength * dx
                force[1] += strength * dy
                force[2] += strength * dz
            for i in range(3):
                total = jnp.sum(force[i], axis=0, keepdims=True) * mine[6]
                pair_out[i, pl.ds(tile, 1)] = total
            return carry

        lax.fori_loop(0, TILES, tile_body, 0)

    def wall_forces(step):
        def tile_body(tile, carry):
            mine = rows_of(own[wall_ids[tile]])
            px, py, pz = [jnp.broadcast_to(r, (8, 128)) for r in mine[0:3]]
            pr = jnp.broadcast_to(mine[6], (8, 128))
            blades = tri[step][wall_picks[tile]].T
            force = [jnp.zeros((8, 128), F32) for _ in range(3)]
            for part in range(16):
                q = blades[8 * part : 8 * part + 8, :]
                nx, ny, nz, cx, cy, cz, narrow, level = [
                    jnp.broadcast_to(q[:, i : i + 1], (8, 128)) for i in range(8)
                ]
                dx, dy, dz = px - cx, py - cy, pz - cz
                height = nx * dx + ny * dy + nz * dz
                window = jnp.maximum(1.0 - (dx * dx + dy * dy + dz * dz) * narrow, 0.0)
                strength = jnp.maximum(pr - jnp.abs(height), 0.0) * height * window
                force[0] += strength * nx
                force[1] += strength * ny
                force[2] += strength * nz
            for i in range(3):
                total = jnp.sum(force[i], axis=0, keepdims=True) * (WALL_STIFF * mine[6])
                wall_out[i, pl.ds(tile, 1)] = total
            return carry

        lax.fori_loop(0, TTILES, tile_body, 0)

    def integrate():
        select = jnp.concatenate([pair_sel[...], wall_sel[...]], axis=0).T[0:NBLK].astype(BF16)
        radius = bodies[6]
        inertia = 1.0 / (radius * radius * radius)
        for i in range(3):
            high, low = split2(jnp.concatenate([pair_out[i], wall_out[i]], axis=0))
            force = jnp.dot(select, high, preferred_element_type=F32)
            force = force + jnp.dot(select, low, preferred_element_type=F32)
            pull = force * inertia
            if i == 2:
                pull = pull - GRAVITY
            velocity = bodies[3 + i] + TIME_STEP * pull
            bodies[3 + i] = velocity
            bodies[i] = bodies[i] + TIME_STEP * velocity

    def send_migrants(step):
        hot = lane_hot[step]
        parts = split3(bodies[...].reshape(7 * NBLK, 128))
        picked = jnp.dot(parts[0], hot, preferred_element_type=F32)
        picked = picked + jnp.dot(parts[1], hot, preferred_element_type=F32)
        picked = picked + jnp.dot(parts[2], hot, preferred_element_type=F32)
        hit = block_hot[step, 0] > 0.5
        for row in range(7):
            line = jnp.where(hit, picked[NBLK * row : NBLK * row + NBLK], 0.0)
            line = jnp.sum(line, axis=0, keepdims=True)
            outgoing[step, 0, row : row + 1, :] = line[:, 0:128]
            outgoing[step, 1, row : row + 1, :] = line[:, 128:256]
        for half in range(2):
            outgoing[step, half, 7:8, :] = jnp.zeros((1, 128), F32)

        def send(hop, carry):
            mig_copy(step, hop).start()
            return carry

        lax.fori_loop(1, GROUP, send, 0)

    def take_migrants(step):
        def wait(hop, carry):
            mig_copy(step, hop).wait_recv()
            return carry

        lax.fori_loop(1, GROUP, wait, 0)
        place = lax.shift_right_logical(lax.broadcasted_iota(jnp.int32, (8, 128), 1), 4)
        shift = (me % 8) * 16
        halves = []
        for half in range(2):
            whole = jnp.zeros((8, 128), F32)
            for spot in range(8):
                turned = pltpu.roll(
                    arrived[step, 8 * half + spot], lax.rem(16 * spot + 128 - shift, 128), axis=1
                )
                whole = jnp.where(place == spot, turned, whole)
            halves.append(whole)
        values = jnp.concatenate(halves, axis=1)
        filled = block_hot[step, 1] > 0.5
        spread = jnp.concatenate(
            [jnp.where(filled, values[row : row + 1, :], 0.0) for row in range(7)], axis=0
        )
        dims = (((1,), (1,)), ((), ()))
        hot = lane_hot[step]
        landed = jnp.zeros((7 * NBLK, 128), F32)
        for part in split3(spread):
            landed = landed + lax.dot_general(part, hot, dims, preferred_element_type=F32)
        hits = lax.dot_general(
            block_hot[step, 1].astype(BF16), hot, dims, preferred_element_type=F32
        )
        for row in range(7):
            bodies[row] = jnp.where(hits > 0.5, landed[NBLK * row : NBLK * row + NBLK], bodies[row])

    for step in range(STEPS):
        for face, (lender, _, _) in enumerate(faces):
            @pl.when(jnp.logical_not(lender))
            def _():
                pool[step][pl.ds(NBLK + GHOST * face, GHOST)] = jnp.zeros((GHOST, 8, 128), F32)
        arrived[step, me] = jnp.zeros((8, 128), F32)

    for load in loads:
        load.wait()
    neighbours = 20 + (gx > 0).astype(jnp.int32) + (gx < SLABS - 1).astype(jnp.int32)
    pl.semaphore_wait(barrier, neighbours)

    for step in range(STEPS):
        send_ghosts(step)
        if step == 0:
            start_tri(0)
            prepare()
            wait_ghosts(0)
            forward_tri(0)
            start_tri(1)
            pair_forces(0)
            finish_tri(0)
            forward_tri(1)
            start_tri(2)
            wait_tri(0)
            wall_forces(0)
            finish_tri(1)
            forward_tri(2)
        else:
            if step == 1:
                wait_tri(1)
            else:
                wait_tri(2)
            wall_forces(step)
            if step == 1:
                finish_tri(2)
            wait_ghosts(step)
            pair_forces(step)
        integrate()
        send_migrants(step)
        take_migrants(step)

    stores = [
        pltpu.make_async_copy(bodies.at[pl.ds(0, 3)], pos_o, in_sem.at[2]),
        pltpu.make_async_copy(bodies.at[pl.ds(3, 3)], vel_o, in_sem.at[3]),
        pltpu.make_async_copy(bodies.at[6], rad_o, in_sem.at[4]),
    ]
    for store in stores:
        store.start()
    for step in range(STEPS):
        for face, (_, borrower, target) in enumerate(faces):
            @pl.when(borrower)
            def _():
                ghost_copy(step, face, target).wait_send()
        zh_copy(step).wait_send()
        for hop in (1, 2, 3):
            x_copy(step, hop).wait_send()
            xz_copy(step, hop).wait_send()
        for slot in range(8):
            core_copy(step, gx, slot).wait_send()

        def wait(hop, carry):
            mig_copy(step, hop).wait_send()
            return carry

        lax.fori_loop(1, GROUP, wait, 0)
    for store in stores:
        store.wait()


def shards(
    position, velocity, radius, vertices, vertex_speed, angles, ghost_blocks,
    tile_home, tile_other, wall_home, wall_block, mig_order, mig_count,
):
    whole = pl.BlockSpec(memory_space=pl.ANY)
    scalars = pl.BlockSpec(memory_space=pltpu.SMEM)
    dma = pltpu.SemaphoreType.DMA
    out = pl.pallas_call(
        kernel,
        out_shape=(
            jax.ShapeDtypeStruct((3, NBLK, 128), F32),
            jax.ShapeDtypeStruct((3, NBLK, 128), F32),
            jax.ShapeDtypeStruct((NBLK, 128), F32),
        ),
        in_specs=[whole] * 6 + [scalars] * 7,
        out_specs=(whole, whole, whole),
        scratch_shapes=[
            pltpu.VMEM((7, NBLK, 128), F32),
            pltpu.VMEM((9, TRIBLK, 128), F32),
            pltpu.VMEM((9, TRIBLK, 128), F32),
            pltpu.VMEM((STEPS, 8, 128), jnp.int32),
            pltpu.VMEM((NBLK, 8, 128), F32),
            *[pltpu.VMEM((POOL, 8, 128), F32) for _ in range(STEPS)],
            pltpu.VMEM((STEPS, GHOST, 8, 128), F32),
            *[pltpu.VMEM((SLABS * TRIBLK, 8, 128), F32) for _ in range(STEPS)],
            pltpu.VMEM((STEPS, 2, 8, 128), F32),
            pltpu.VMEM((STEPS, GROUP, 8, 128), F32),
            pltpu.VMEM((STEPS, 128, 256), BF16),
            pltpu.VMEM((STEPS, 2, NBLK, 256), F32),
            pltpu.VMEM((TILES, 128), F32),
            pltpu.VMEM((TTILES, 128), F32),
            pltpu.VMEM((3, TILES, 128), F32),
            pltpu.VMEM((3, TTILES, 128), F32),
            dma((6,)),
            dma((STEPS, 6)),
            dma((STEPS, 6)),
            dma((STEPS, GROUP)),
            dma((STEPS, GROUP)),
            dma((STEPS,)),
            dma((STEPS,)),
            dma((STEPS, 3)),
            dma((STEPS, 3)),
            dma((STEPS, 3)),
            dma((STEPS, 3)),
            dma((STEPS, 8)),
            dma((STEPS, 8)),
        ],
        compiler_params=pltpu.CompilerParams(
            collective_id=0, has_side_effects=True, vmem_limit_bytes=32 * 1024 * 1024
        ),
    )(
        position.reshape(3, NBLK, 128),
        velocity.reshape(3, NBLK, 128),
        radius.reshape(NBLK, 128),
        vertices.reshape(9, TRIBLK, 128),
        vertex_speed.reshape(9, TRIBLK, 128),
        mig_order.reshape(STEPS, NBLK, 128),
        angles,
        ghost_blocks.reshape(-1),
        tile_home.reshape(-1),
        tile_other.reshape(-1),
        wall_home.reshape(-1),
        wall_block.reshape(-1),
        mig_count.reshape(STEPS, GROUP),
    )
    return (
        out[0].reshape(position.shape),
        out[1].reshape(velocity.shape),
        out[2].reshape(radius.shape),
    )


def solution(mesh):
    block = P("gx", "gy", "gz", None)
    blocks = P(None, "gx", "gy", "gz", None)
    in_specs = (
        blocks, blocks, block, blocks, blocks, P(), block, block, block, block, block, blocks, blocks,
    )
    return jax.shard_map(
        shards, mesh=mesh, in_specs=in_specs, out_specs=(blocks, blocks, block), check_vma=False
    )
```

profile of v0, /device:TPU:1, one launch (start us, length us, event | category | flops | bytes accessed | tf_op | source)
XLA Modules:
  0.0 154.6 jit_solution(12526372332216513628)
XLA Ops:
  0.6 0.0 copy-start.5
  0.6 0.0 copy-start.12
  0.7 0.7 copy-done.12
  1.3 0.0 copy-start.9
  1.3 0.0 copy-start.10
  1.3 0.0 copy-start.11
  1.3 0.0 copy-start.6
  1.4 0.0 copy-start.7
  1.4 0.0 copy-start.8
  1.4 0.0 copy-done.5
  1.4 0.6 copy-done.9
  2.0 0.0 copy-done.10
  2.0 0.0 copy-done.11
  2.0 0.0 copy-done.6
  2.0 0.0 copy-done.7
  2.0 0.0 copy-done.8
  2.1 0.0 copy-start
  2.1 0.9 copy-done
  2.9 0.0 copy-start.1
  3.0 0.9 copy-done.1
  3.8 0.0 copy-start.2
  3.8 0.8 copy-done.2
  4.6 0.0 copy-start.3
  4.6 0.8 copy-done.3
  5.4 0.0 copy-start.4
  5.4 0.8 copy-done.4
  6.2 146.5 %shard_map.148 = (f32[3,32,128]{2,1,0:T(8,128)S(1)}, f32[3,32,128]{2,1,0:T(8,128)S(1)}, f32[32,128]{1,0:T(8,128)S(1)}) custom-call(f32[3,32,128]{2,1,0:T(8,128)S(1)} %bitcast.19, f32[3,32,128]{2,1,0:T(8,128)S(1)} %bitcast.20, f32[32,128]{1,0:T(8,128)S(1)} %bitcast.24, f32[9,16,128]{2,1,0:T(8,128)S(1)} %bitcast.17, f32[9,16,128]{2,1,0:T(8,128)S(1)} %bitcast.18, ...), custom_call_target="tpu_custom_call" | custom-call | tf_op jit(solution)/shard_map/pallas_call | solution.py:464
  152.8 0.6 copy.26
  153.4 0.6 copy.27
  154.0 0.6 copy.28
  (1 shorter events, 0.0 us)
Async XLA Ops:
  0.6 0.7 copy-start.5
  0.6 0.7 copy-start.12
  1.3 0.7 copy-start.9
  1.3 0.7 copy-start.10
  1.3 0.7 copy-start.11
  1.3 0.7 copy-start.6
  1.4 0.7 copy-start.7
  1.4 0.7 copy-start.8
  2.1 0.9 copy-start
  2.9 0.9 copy-start.1
  3.8 0.8 copy-start.2
  4.6 0.8 copy-start.3
  5.4 0.8 copy-start.4
where the time goes:
time: 155 us
  Pallas kernels  147 us (95%)
  local copies, waits for them, and re-layouts  7.38 us (5%)
    pallas_call x1, Pallas kernels, shards(): pl.pallas_call(kernel, out_shape=(jax.ShapeDtypeStruct((3, NBLK, 128), F3...  147 us
    unnamed x30, local copies, waits for them, and re-layouts  7.38 us

commit v1 on v0

--- a/solution.py
+++ b/solution.py
@@ -21,6 +21,7 @@
 SLABS = 16
 GROUP = 16
 MC = 16
+SOME = 8
 
 STIFFNESS = 20.0
 DAMPING = 2.0
@@ -47,8 +48,123 @@
     return high, low
 
 
-def rows_of(block):
-    return [block[i : i + 1, :] for i in range(8)]
+def split3_wide(values):
+    high = values.astype(BF16).astype(F32)
+    rest = values - high
+    middle = rest.astype(BF16).astype(F32)
+    return high, middle, rest - middle
+
+
+def swapped(block, row):
+    return jnp.where(row < 3, pltpu.roll(block, 5, axis=0), pltpu.roll(block, 3, axis=0))
+
+
+def over_rows(values, mask):
+    total = jnp.sum(jnp.where(mask, values, 0.0), axis=0, keepdims=True)
+    return jnp.broadcast_to(total, (8, 128))
+
+
+def by_row(row, values):
+    out = values[-1]
+    for i in range(len(values) - 2, -1, -1):
+        out = jnp.where(row == i, values[i], out)
+    return out
+
+
+def stacked(groups):
+    return jnp.concatenate(groups, axis=0)
+
+
+def anchor_of(home, row):
+    return jnp.where(row < 6, jnp.broadcast_to(home[:, 0:1], (8, 128)), 0.0)
+
+
+def pair_home(home, row):
+    block = home - anchor_of(home, row)
+    turned = swapped(block, row)
+    norm = split3_wide(over_rows(block * block, row < 3) + SOFTENING)
+    drift = split3_wide(-DAMPING * over_rows(block * turned, row < 3))
+    size = split3_wide(jnp.broadcast_to(block[6:7], (8, 128)))
+    zero, one = jnp.zeros((8, 128), F32), jnp.ones((8, 128), F32)
+    near = [jnp.where(row < 3, -2.0 * part, 0.0) for part in split3_wide(block)]
+    cross = [jnp.where(row < 6, DAMPING * part, 0.0) for part in split3_wide(turned)]
+    six = (row == 6).astype(F32)
+    near_end = by_row(row, [one, one, one, zero, zero, norm[0], norm[1], norm[2]])
+    cross_end = by_row(
+        row, [zero, zero, zero, -DAMPING * one, -DAMPING * one, drift[0], drift[1], drift[2]]
+    )
+    size_end = by_row(row, [zero, zero, zero, zero, zero, size[0], size[1], size[2]])
+    return jnp.concatenate(
+        [
+            stacked([near[0], near[1], near[0], near[1], near[2], near[0], near_end, zero]),
+            stacked([cross[0], cross[1], cross[0], cross[1], cross[2], cross[0], cross_end, zero]),
+            stacked([six, zero, six, zero, zero, six, size_end, zero]),
+        ],
+        axis=1,
+    ).astype(BF16)
+
+
+def low_below(weights, row):
+    high = weights.astype(BF16).astype(F32)
+    return jnp.where(row < 4, high, pltpu.roll(weights - high, 4, axis=0)).astype(BF16)
+
+
+def pair_other(other, home, row):
+    block = other - anchor_of(home, row)
+    turned = swapped(block, row)
+    norm = split3_wide(over_rows(block * block, row < 3))
+    drift = over_rows(block * turned, row < 3)
+    drift_high = drift.astype(BF16).astype(F32)
+    one = jnp.ones((8, 128), F32)
+    end = by_row(row, [norm[0], norm[1], norm[2], drift_high, drift - drift_high, one, one, one])
+    part = split3_wide(block)
+    left = stacked(
+        [part[0], part[0], part[1], part[1], part[0], part[2], end, jnp.zeros((8, 128), F32)]
+    ).astype(BF16)
+    weights = jnp.where(row < 3, block, 1.0) * jnp.broadcast_to(block[6:7], (8, 128))
+    return left, low_below(weights, row)
+
+
+def wall_home(home, row):
+    block = home - AXIS_CENTRE
+    norm = split3_wide(-over_rows(block * block, row < 3))
+    parts = split3_wide(block)
+    zero = jnp.zeros((8, 128), F32)
+    high = [jnp.where(row < 3, part, 0.0) for part in parts]
+    wide = [
+        jnp.where(jnp.logical_and(row >= 3, row < 6), 2.0 * pltpu.roll(part, 3, axis=0), 0.0)
+        for part in parts
+    ]
+    level = jnp.where(row == 7, -1.0, 0.0)
+    six = (row == 6).astype(F32)
+    end = by_row(row, [norm[0], norm[1], norm[2], zero])
+    return jnp.concatenate(
+        [
+            stacked([high[0] + level, high[1], high[0] + level, high[1], high[2], high[0] + level, zero, zero]),
+            stacked([wide[0] + six, wide[1], wide[0] + six, wide[1], wide[2], wide[0] + six, end, zero]),
+        ],
+        axis=1,
+    ).astype(BF16)
+
+
+def wall_other(blades, row):
+    part = split3_wide(blades)
+    end = jnp.where(row < 3, 1.0, 0.0)
+    left = stacked(
+        [part[0], part[0], part[1], part[1], part[0], part[2], end, jnp.zeros((8, 128), F32)]
+    ).astype(BF16)
+    reach = over_rows(blades * blades, jnp.logical_and(row >= 3, row < 6))
+    weights = blades / (reach + jnp.broadcast_to(blades[6:7], (8, 128)))
+    return left, low_below(weights, row)
+
+
+def weighted(weights, strength):
+    high, low = split2(strength)
+    return jnp.dot(
+        jnp.concatenate([weights, weights], axis=1),
+        jnp.concatenate([high, low], axis=0),
+        preferred_element_type=F32,
+    )
 
 
 def kernel(
@@ -58,6 +174,7 @@
     bodies, corners, speeds, order, own, pool_0, pool_1, pool_2, lent, tri_0, tri_1, tri_2,
     outgoing, arrived, lane_hot, block_hot,
     pair_sel, wall_sel, pair_out, wall_out,
+    pair_right, pair_left, pair_weight, wall_right, wall_left, wall_weight,
     in_sem, ghost_send, ghost_recv, mig_send, mig_recv,
     zh_send, zh_recv, x_send, x_recv, xz_send, xz_recv, core_send, core_recv,
 ):
@@ -156,12 +273,14 @@
             device_id_type=MESH,
         )
 
-    def send_ghosts(step):
+    def lend(step):
         for row in range(7):
             own[:, row, :] = bodies[row]
         own[:, 7, :] = jnp.zeros((NBLK, 128), F32)
         for slot in range(GHOST):
             lent[step, slot] = own[ghost_ids[slot]]
+
+    def send_ghosts(step):
         for face, (_, borrower, target) in enumerate(faces):
             @pl.when(borrower)
             def _():
@@ -207,13 +326,14 @@
         for corner in (a, b, c):
             for i in range(3):
                 spread = spread + (corner[i] - centre[i]) ** 2 * (1.0 / 3.0)
-        level = normal[0] * centre[0] + normal[1] * centre[1] + normal[2] * centre[2]
-        rows = normal + centre + [1.0 / spread, level]
+        shifted = [centre[i] - AXIS_CENTRE for i in range(3)]
+        square = shifted[0] ** 2 + shifted[1] ** 2 + shifted[2] ** 2
+        level = normal[0] * shifted[0] + normal[1] * shifted[1] + normal[2] * shifted[2]
+        rows = normal + shifted + [spread - square, level]
         for row in range(8):
             tri[step][pl.ds(gx * TRIBLK, TRIBLK), row, :] = rows[row]
 
     def start_tri(step):
-        blade_move(step)
         zh_copy(step).start()
         core_copy(step, gx, 0).start()
         for hop in (1, 2, 3):
@@ -246,89 +366,108 @@
             lane_hot[step] = (jnp.bitwise_and(ids, 127) == lane).astype(F32).astype(BF16)
             limit = jnp.zeros((1, 256), jnp.int32)
             for peer in range(GROUP):
-                limit = jnp.where(lax.shift_right_logical(place, 4) == peer, counts[step, peer], limit)
+                limit = jnp.where(lax.shift_right_logical(place, 4) == peer, counts[step, 0, peer], limit)
             filled = jnp.bitwise_and(place, 15) < limit
             hot = lax.shift_right_logical(ids, 7) == block
             block_hot[step, 0] = hot.astype(F32)
             block_hot[step, 1] = jnp.logical_and(hot, filled).astype(F32)
         home = lax.broadcasted_iota(jnp.int32, (1, 128), 1)
-        for tile in range(TILES):
-            pair_sel[pl.ds(tile, 1)] = (home == home_ids[tile]).astype(F32)
-        for tile in range(TTILES):
-            wall_sel[pl.ds(tile, 1)] = (home == wall_ids[tile]).astype(F32)
+        hot = [(home == home_ids[tile]).astype(F32) for tile in range(TILES)]
+        pair_sel[...] = stacked(hot).T[0:NBLK].astype(BF16)
+        hot = [(home == wall_ids[tile]).astype(F32) for tile in range(TTILES)]
+        wall_sel[...] = stacked(hot).T[0:NBLK].astype(BF16)
+
+    def pair_homes():
+        def some(turn, carry):
+            row = lax.broadcasted_iota(jnp.int32, (8, 128), 0)
+            for spot in range(SOME):
+                tile = turn * SOME + spot
+                pair_right[tile] = pair_home(own[home_ids[tile]], row)
+            return carry
+
+        lax.fori_loop(0, TILES // SOME, some, 0)
 
     def pair_forces(step):
-        def tile_body(tile, carry):
-            mine = rows_of(own[home_ids[tile]])
-            px, py, pz, pu, pv, pw, pr, _ = [jnp.broadcast_to(r, (8, 128)) for r in mine]
-            theirs = pool[step][other_ids[tile]].T
-            force = [jnp.zeros((8, 128), F32) for _ in range(3)]
-            for part in range(16):
-                q = theirs[8 * part : 8 * part + 8, :]
-                qx, qy, qz, qu, qv, qw, qr = [
-                    jnp.broadcast_to(q[:, i : i + 1], (8, 128)) for i in range(7)
-                ]
-                dx, dy, dz = px - qx, py - qy, pz - qz
-                square = dx * dx + dy * dy + dz * dz + SOFTENING
-                speed = (pu - qu) * dx + (pv - qv) * dy + (pw - qw) * dz
-                reach = pr + qr
+        def features(turn, carry):
+            row = lax.broadcasted_iota(jnp.int32, (8, 128), 0)
+            for spot in range(SOME):
+                tile = turn * SOME + spot
+                left, weights = pair_other(pool[step][other_ids[tile]], own[home_ids[tile]], row)
+                pair_left[tile] = left.T
+                pair_weight[tile] = weights
+            return carry
+
+        def forces(turn, carry):
+            tiles = [turn * SOME + spot for spot in range(SOME)]
+            forms = [
+                jnp.dot(pair_left[tile], pair_right[tile], preferred_element_type=F32)
+                for tile in tiles
+            ]
+            strengths = []
+            for form in forms:
+                square = jnp.maximum(form[:, 0:128], SOFTENING)
+                speed, reach = form[:, 128:256], form[:, 256:384]
                 scaled = square * reach
                 ratio = lax.rsqrt(scaled * reach)
-                dist = scaled * ratio
-                over = reach * ratio
-                overlap = jnp.maximum(reach - dist, 0.0)
-                factor = STIFFNESS - (DAMPING * speed) * over
-                strength = qr * ratio * overlap * factor
-                force[0] += strength * dx
-                force[1] += strength * dy
-                force[2] += strength * dz
-            for i in range(3):
-                total = jnp.sum(force[i], axis=0, keepdims=True) * mine[6]
-                pair_out[i, pl.ds(tile, 1)] = total
-            return carry
-
-        lax.fori_loop(0, TILES, tile_body, 0)
+                overlap = jnp.maximum(reach - scaled * ratio, 0.0)
+                strengths.append(overlap * ratio * (STIFFNESS + speed * (reach * ratio)))
+            for tile, strength in zip(tiles, strengths):
+                pair_out[tile] = weighted(pair_weight[tile], strength)
+            return carry
+
+        lax.fori_loop(0, TILES // SOME, features, 0)
+        lax.fori_loop(0, TILES // SOME, forces, 0)
 
     def wall_forces(step):
-        def tile_body(tile, carry):
-            mine = rows_of(own[wall_ids[tile]])
-            px, py, pz = [jnp.broadcast_to(r, (8, 128)) for r in mine[0:3]]
-            pr = jnp.broadcast_to(mine[6], (8, 128))
-            blades = tri[step][wall_picks[tile]].T
-            force = [jnp.zeros((8, 128), F32) for _ in range(3)]
-            for part in range(16):
-                q = blades[8 * part : 8 * part + 8, :]
-                nx, ny, nz, cx, cy, cz, narrow, level = [
-                    jnp.broadcast_to(q[:, i : i + 1], (8, 128)) for i in range(8)
-                ]
-                dx, dy, dz = px - cx, py - cy, pz - cz
-                height = nx * dx + ny * dy + nz * dz
-                window = jnp.maximum(1.0 - (dx * dx + dy * dy + dz * dz) * narrow, 0.0)
-                strength = jnp.maximum(pr - jnp.abs(height), 0.0) * height * window
-                force[0] += strength * nx
-                force[1] += strength * ny
-                force[2] += strength * nz
-            for i in range(3):
-                total = jnp.sum(force[i], axis=0, keepdims=True) * (WALL_STIFF * mine[6])
-                wall_out[i, pl.ds(tile, 1)] = total
-            return carry
-
-        lax.fori_loop(0, TTILES, tile_body, 0)
+        def features(turn, carry):
+            row = lax.broadcasted_iota(jnp.int32, (8, 128), 0)
+            for spot in range(SOME):
+                tile = turn * SOME + spot
+                wall_right[tile] = wall_home(own[wall_ids[tile]], row)
+                left, weights = wall_other(tri[step][wall_picks[tile]], row)
+                wall_left[tile] = left.T
+                wall_weight[tile] = weights
+            return carry
+
+        def forces(turn, carry):
+            tiles = [turn * SOME + spot for spot in range(SOME)]
+            forms = [
+                jnp.dot(wall_left[tile], wall_right[tile], preferred_element_type=F32)
+                for tile in tiles
+            ]
+            strengths = []
+            for tile, form in zip(tiles, forms):
+                radius = own[wall_ids[tile]][6:7, :]
+                height, window = form[:, 0:128], form[:, 128:256]
+                depth = jnp.maximum(radius - jnp.abs(height), 0.0)
+                strengths.append(depth * height * jnp.maximum(window, 0.0))
+            for tile, strength in zip(tiles, strengths):
+                wall_out[tile] = weighted(wall_weight[tile], strength)
+            return carry
+
+        lax.fori_loop(0, TTILES // SOME, features, 0)
+        lax.fori_loop(0, TTILES // SOME, forces, 0)
 
     def integrate():
-        select = jnp.concatenate([pair_sel[...], wall_sel[...]], axis=0).T[0:NBLK].astype(BF16)
+        def home_sum(select, out, row):
+            high, low = split2(out[:, row, :] + out[:, row + 4, :])
+            return jnp.dot(select, high, preferred_element_type=F32) + jnp.dot(
+                select, low, preferred_element_type=F32
+            )
+
+        pairs, walls = pair_sel[...], wall_sel[...]
+        weight = home_sum(pairs, pair_out, 3)
         radius = bodies[6]
-        inertia = 1.0 / (radius * radius * radius)
+        inertia = 1.0 / (radius * radius)
         for i in range(3):
-            high, low = split2(jnp.concatenate([pair_out[i], wall_out[i]], axis=0))
-            force = jnp.dot(select, high, preferred_element_type=F32)
-            force = force + jnp.dot(select, low, preferred_element_type=F32)
-            pull = force * inertia
+            place = bodies[i]
+            contact = (place - place[:, 0:1]) * weight - home_sum(pairs, pair_out, i)
+            pull = (contact + WALL_STIFF * home_sum(walls, wall_out, i)) * inertia
             if i == 2:
                 pull = pull - GRAVITY
             velocity = bodies[3 + i] + TIME_STEP * pull
             bodies[3 + i] = velocity
-            bodies[i] = bodies[i] + TIME_STEP * velocity
+            bodies[i] = place + TIME_STEP * velocity
 
     def send_migrants(step):
         hot = lane_hot[step]
@@ -393,17 +532,24 @@
 
     for load in loads:
         load.wait()
+    lend(0)
+    blade_move(0)
     neighbours = 20 + (gx > 0).astype(jnp.int32) + (gx < SLABS - 1).astype(jnp.int32)
     pl.semaphore_wait(barrier, neighbours)
 
     for step in range(STEPS):
+        if step > 0:
+            lend(step)
         send_ghosts(step)
         if step == 0:
             start_tri(0)
+            pair_homes()
+            blade_move(1)
+            blade_move(2)
             prepare()
-            wait_ghosts(0)
             forward_tri(0)
             start_tri(1)
+            wait_ghosts(0)
             pair_forces(0)
             finish_tri(0)
             forward_tri(1)
@@ -413,10 +559,8 @@
             finish_tri(1)
             forward_tri(2)
         else:
-            if step == 1:
-                wait_tri(1)
-            else:
-                wait_tri(2)
+            pair_homes()
+            wait_tri(step)
             wall_forces(step)
             if step == 1:
                 finish_tri(2)
@@ -483,10 +627,16 @@
             pltpu.VMEM((STEPS, GROUP, 8, 128), F32),
             pltpu.VMEM((STEPS, 128, 256), BF16),
             pltpu.VMEM((STEPS, 2, NBLK, 256), F32),
-            pltpu.VMEM((TILES, 128), F32),
-            pltpu.VMEM((TTILES, 128), F32),
-            pltpu.VMEM((3, TILES, 128), F32),
-            pltpu.VMEM((3, TTILES, 128), F32),
+            pltpu.VMEM((NBLK, TILES), BF16),
+            pltpu.VMEM((NBLK, TTILES), BF16),
+            pltpu.VMEM((TILES, 8, 128), F32),
+            pltpu.VMEM((TTILES, 8, 128), F32),
+            pltpu.VMEM((TILES, 64, 384), BF16),
+            pltpu.VMEM((TILES, 128, 64), BF16),
+            pltpu.VMEM((TILES, 8, 128), BF16),
+            pltpu.VMEM((TTILES, 64, 256), BF16),
+            pltpu.VMEM((TTILES, 128, 64), BF16),
+            pltpu.VMEM((TTILES, 8, 128), BF16),
             dma((6,)),
             dma((STEPS, 6)),
             dma((STEPS, 6)),
@@ -502,7 +652,7 @@
             dma((STEPS, 8)),
         ],
         compiler_params=pltpu.CompilerParams(
-            collective_id=0, has_side_effects=True, vmem_limit_bytes=32 * 1024 * 1024
+            collective_id=0, has_side_effects=True, vmem_limit_bytes=60 * 1024 * 1024
         ),
     )(
         position.reshape(3, NBLK, 128),
@@ -517,7 +667,7 @@
         tile_other.reshape(-1),
         wall_home.reshape(-1),
         wall_block.reshape(-1),
-        mig_count.reshape(STEPS, GROUP),
+        mig_count.reshape(STEPS, 1, GROUP),
     )
     return (
         out[0].reshape(position.shape),

time: 155 us -> 83.4 us (0.54)
  Pallas kernels: 147 us -> 78.7 us
  local copies, waits for them, and re-layouts: 7.38 us -> 2.76 us
    pallas_call x1, Pallas kernels: 147 us -> 78.7 us  [shards(): pl.pallas_call(kernel, out_shape=(jax.ShapeDtypeStruct((3, NBLK, 128), F3...]
    unnamed x30 -> x7, local copies, waits for them, and re-layouts: 7.38 us -> 2.76 us
where the time goes in v1:
time: 83.4 us; the launch traced here: 82.1 us
  Pallas kernels  78.7 us (94%)
  local copies, waits for them, and re-layouts  2.76 us (3%)
    pallas_call x1, Pallas kernels, shards(): pl.pallas_call(kernel, out_shape=(jax.ShapeDtypeStruct((3, NBLK, 128), F3...  78.7 us
    unnamed x7, local copies, waits for them, and re-layouts  2.76 us

profile of v1, /device:TPU:1, one launch (start us, length us, event | category | flops | bytes accessed | tf_op | source)
XLA Modules:
  0.0 82.1 jit_solution(16113866133791176918)
XLA Ops:
  0.6 78.7 %shard_map.148 = (f32[3,32,128]{2,1,0:T(8,128)}, f32[3,32,128]{2,1,0:T(8,128)}, f32[32,128]{1,0:T(8,128)}) custom-call(f32[3,32,128]{2,1,0:T(8,128)} %bitcast.17, f32[3,32,128]{2,1,0:T(8,128)} %bitcast.18, f32[32,128]{1,0:T(8,128)} %bitcast.22, f32[9,16,128]{2,1,0:T(8,128)} %bitcast.15, f32[9,16,128]{2,1,0:T(8,128)} %bitcast.16, s32[3,32,128]{2,1,0:T(8,128)} %bitcast.19, ...), custom_call_target="tpu_custom_call" | custom-call | tf_op jit(solution)/shard_map/pallas_call | solution.py:608
  79.4 0.0 copy-start
  79.4 1.4 %copy.23 = f32[3,1,1,1,4096]{4,3,2,1,0:T(1,128)} copy(f32[3,1,1,1,4096]{4,3,2,1,0:T(1,128)} %bitcast.21) | data formatting | bytes 98304
  80.8 0.0 copy-done
  80.8 0.0 copy-start.1
  80.8 0.6 copy.24
  81.4 0.1 copy-done.1
  81.5 0.6 copy.25
Async XLA Ops:
  79.4 1.4 %copy-start = (f32[3,32,128]{2,1,0:T(8,128)S(1)}, f32[3,32,128]{2,1,0:T(8,128)}, u32[]{:S(2)}) copy-start(f32[3,32,128]{2,1,0:T(8,128)} %get-tuple-element.7) | copy-start | bytes 147460
  80.8 0.7 copy-start.1

commit v2 on v1

--- a/solution.py
+++ b/solution.py
@@ -21,7 +21,7 @@
 SLABS = 16
 GROUP = 16
 MC = 16
-SOME = 8
+SOME = 32
 
 STIFFNESS = 20.0
 DAMPING = 2.0
@@ -199,8 +199,8 @@
         load.start()
 
     def peer_of(hop):
-        peer = lax.rem(me + hop, GROUP)
-        return peer, (gx, peer // 4, peer % 4)
+        row, column = lax.rem(gy + hop // 4, 4), lax.rem(gz + hop % 4, 4)
+        return row * 4 + column, (gx, row, column)
 
     def x_mate(hop, z_of):
         index = lax.rem(x_at + hop, 4) * 4 + z_of * 2 + core
@@ -334,7 +334,6 @@
             tri[step][pl.ds(gx * TRIBLK, TRIBLK), row, :] = rows[row]
 
     def start_tri(step):
-        zh_copy(step).start()
         core_copy(step, gx, 0).start()
         for hop in (1, 2, 3):
             x_copy(step, hop).start()
@@ -345,10 +344,12 @@
             xz_copy(step, hop).start()
         core_copy(step, zmate, 1).start()
 
-    def finish_tri(step):
+    def pass_near(step):
         for hop in (1, 2, 3):
             x_copy(step, hop).wait_recv()
             core_copy(step, x_mate(4 - hop, zh), 1 + hop).start()
+
+    def pass_far(step):
         for hop in (1, 2, 3):
             xz_copy(step, hop).wait_recv()
             core_copy(step, x_mate(4 - hop, 1 - zh), 4 + hop).start()
@@ -387,7 +388,7 @@
 
         lax.fori_loop(0, TILES // SOME, some, 0)
 
-    def pair_forces(step):
+    def pair_features(step):
         def features(turn, carry):
             row = lax.broadcasted_iota(jnp.int32, (8, 128), 0)
             for spot in range(SOME):
@@ -397,6 +398,9 @@
                 pair_weight[tile] = weights
             return carry
 
+        lax.fori_loop(0, TILES // SOME, features, 0)
+
+    def pair_forces(first, last):
         def forces(turn, carry):
             tiles = [turn * SOME + spot for spot in range(SOME)]
             forms = [
@@ -415,20 +419,31 @@
                 pair_out[tile] = weighted(pair_weight[tile], strength)
             return carry
 
-        lax.fori_loop(0, TILES // SOME, features, 0)
-        lax.fori_loop(0, TILES // SOME, forces, 0)
-
-    def wall_forces(step):
+        lax.fori_loop(first, last, forces, 0)
+
+    def wall_homes():
+        def some(turn, carry):
+            row = lax.broadcasted_iota(jnp.int32, (8, 128), 0)
+            for spot in range(SOME):
+                tile = turn * SOME + spot
+                wall_right[tile] = wall_home(own[wall_ids[tile]], row)
+            return carry
+
+        lax.fori_loop(0, TTILES // SOME, some, 0)
+
+    def wall_features(step):
         def features(turn, carry):
             row = lax.broadcasted_iota(jnp.int32, (8, 128), 0)
             for spot in range(SOME):
                 tile = turn * SOME + spot
-                wall_right[tile] = wall_home(own[wall_ids[tile]], row)
                 left, weights = wall_other(tri[step][wall_picks[tile]], row)
                 wall_left[tile] = left.T
                 wall_weight[tile] = weights
             return carry
 
+        lax.fori_loop(0, TTILES // SOME, features, 0)
+
+    def wall_forces():
         def forces(turn, carry):
             tiles = [turn * SOME + spot for spot in range(SOME)]
             forms = [
@@ -445,7 +460,6 @@
                 wall_out[tile] = weighted(wall_weight[tile], strength)
             return carry
 
-        lax.fori_loop(0, TTILES // SOME, features, 0)
         lax.fori_loop(0, TTILES // SOME, forces, 0)
 
     def integrate():
@@ -484,11 +498,10 @@
         for half in range(2):
             outgoing[step, half, 7:8, :] = jnp.zeros((1, 128), F32)
 
-        def send(hop, carry):
-            mig_copy(step, hop).start()
-            return carry
-
-        lax.fori_loop(1, GROUP, send, 0)
+        for along in (2, 1, 3, 0):
+            for across in (1, 3, 2, 0):
+                if along or across:
+                    mig_copy(step, 4 * across + along).start()
 
     def take_migrants(step):
         def wait(hop, carry):
@@ -538,45 +551,55 @@
     pl.semaphore_wait(barrier, neighbours)
 
     for step in range(STEPS):
-        if step > 0:
+        if step == 0:
+            zh_copy(0).start()
+        else:
             lend(step)
         send_ghosts(step)
         if step == 0:
             start_tri(0)
             pair_homes()
             blade_move(1)
+            pass_near(0)
+            forward_tri(0)
             blade_move(2)
+            wall_homes()
             prepare()
-            forward_tri(0)
+            wait_ghosts(0)
+            pair_features(0)
+            pair_forces(0, 1)
+            pass_far(0)
+            zh_copy(1).start()
             start_tri(1)
-            wait_ghosts(0)
-            pair_forces(0)
-            finish_tri(0)
-            forward_tri(1)
-            start_tri(2)
+            pair_forces(1, 2)
             wait_tri(0)
-            wall_forces(0)
-            finish_tri(1)
-            forward_tri(2)
+            wall_features(0)
+            wall_forces()
         else:
+            wall_homes()
             pair_homes()
+            pass_far(step)
+            if step == 1:
+                forward_tri(2)
+                pass_near(2)
             wait_tri(step)
-            wall_forces(step)
-            if step == 1:
-                finish_tri(2)
+            wall_features(step)
+            wall_forces()
             wait_ghosts(step)
-            pair_forces(step)
+            pair_features(step)
+            pair_forces(0, 2)
         integrate()
         send_migrants(step)
+        if step == 0:
+            pass_near(1)
+            forward_tri(1)
+            zh_copy(2).start()
+            start_tri(2)
         take_migrants(step)
 
-    stores = [
-        pltpu.make_async_copy(bodies.at[pl.ds(0, 3)], pos_o, in_sem.at[2]),
-        pltpu.make_async_copy(bodies.at[pl.ds(3, 3)], vel_o, in_sem.at[3]),
-        pltpu.make_async_copy(bodies.at[6], rad_o, in_sem.at[4]),
-    ]
-    for store in stores:
-        store.start()
+    pos_o[...] = bodies[0:3]
+    vel_o[...] = bodies[3:6]
+    rad_o[...] = bodies[6]
     for step in range(STEPS):
         for face, (_, borrower, target) in enumerate(faces):
             @pl.when(borrower)
@@ -594,8 +617,6 @@
             return carry
 
         lax.fori_loop(1, GROUP, wait, 0)
-    for store in stores:
-        store.wait()
 
 
 def shards(
@@ -604,16 +625,17 @@
 ):
     whole = pl.BlockSpec(memory_space=pl.ANY)
     scalars = pl.BlockSpec(memory_space=pltpu.SMEM)
+    here = pl.BlockSpec(memory_space=pltpu.VMEM)
     dma = pltpu.SemaphoreType.DMA
     out = pl.pallas_call(
         kernel,
         out_shape=(
-            jax.ShapeDtypeStruct((3, NBLK, 128), F32),
-            jax.ShapeDtypeStruct((3, NBLK, 128), F32),
-            jax.ShapeDtypeStruct((NBLK, 128), F32),
+            pltpu.VMEM((3, NBLK, 128), F32),
+            pltpu.VMEM((3, NBLK, 128), F32),
+            pltpu.VMEM((NBLK, 128), F32),
         ),
         in_specs=[whole] * 6 + [scalars] * 7,
-        out_specs=(whole, whole, whole),
+        out_specs=(here, here, here),
         scratch_shapes=[
             pltpu.VMEM((7, NBLK, 128), F32),
             pltpu.VMEM((9, TRIBLK, 128), F32),

time: 83.4 us -> 70 us (0.84); the launches traced: 82.1 us -> 69.8 us
  Pallas kernels: 78.7 us -> 67.3 us
  local copies, waits for them, and re-layouts: 2.76 us -> 1.85 us
    pallas_call x1, Pallas kernels: 78.7 us -> 67.3 us  [shards(): pl.pallas_call(kernel, out_shape=(pltpu.VMEM((3, NBLK, 128), F32), pltpu....]
    unnamed x7 -> x3, local copies, waits for them, and re-layouts: 2.76 us -> 1.85 us
where the time goes in v2:
time: 70 us; the launch traced here: 69.8 us
  Pallas kernels  67.3 us (96%)
  local copies, waits for them, and re-layouts  1.85 us (3%)
    pallas_call x1, Pallas kernels, shards(): pl.pallas_call(kernel, out_shape=(pltpu.VMEM((3, NBLK, 128), F32), pltpu....  67.3 us
    unnamed x3, local copies, waits for them, and re-layouts  1.85 us

profile of v2, /device:TPU:1, one launch (start us, length us, event | category | flops | bytes accessed | tf_op | source)
XLA Modules:
  0.0 69.8 jit_solution(17176344671956690747)
XLA Ops:
  0.6 67.3 %shard_map.148 = (f32[3,32,128]{2,1,0:T(8,128)S(1)}, f32[3,32,128]{2,1,0:T(8,128)S(1)}, f32[32,128]{1,0:T(8,128)S(1)}) custom-call(f32[3,32,128]{2,1,0:T(8,128)} %bitcast.20, f32[3,32,128]{2,1,0:T(8,128)} %bitcast.21, f32[32,128]{1,0:T(8,128)} %bitcast.23, f32[9,16,128]{2,1,0:T(8,128)} %bitcast.18, f32[9,16,128]{2,1,0:T(8,128)} %bitcast.19, ...), custom_call_target="tpu_custom_call" | custom-call | tf_op jit(solution)/shard_map/pallas_call | solution.py:630
  68.0 0.6 copy.23
  68.6 0.6 copy.24
  69.2 0.6 copy.25

commit v3 on v2

--- a/solution.py
+++ b/solution.py
@@ -22,6 +22,7 @@
 GROUP = 16
 MC = 16
 SOME = 32
+SOON = 8
 
 STIFFNESS = 20.0
 DAMPING = 2.0
@@ -174,7 +175,7 @@
     bodies, corners, speeds, order, own, pool_0, pool_1, pool_2, lent, tri_0, tri_1, tri_2,
     outgoing, arrived, lane_hot, block_hot,
     pair_sel, wall_sel, pair_out, wall_out,
-    pair_right, pair_left, pair_weight, wall_right, wall_left, wall_weight,
+    pair_right, wall_right, wall_left, wall_weight,
     in_sem, ghost_send, ghost_recv, mig_send, mig_recv,
     zh_send, zh_recv, x_send, x_recv, xz_send, xz_recv, core_send, core_recv,
 ):
@@ -388,38 +389,32 @@
 
         lax.fori_loop(0, TILES // SOME, some, 0)
 
-    def pair_features(step):
-        def features(turn, carry):
-            row = lax.broadcasted_iota(jnp.int32, (8, 128), 0)
-            for spot in range(SOME):
-                tile = turn * SOME + spot
-                left, weights = pair_other(pool[step][other_ids[tile]], own[home_ids[tile]], row)
-                pair_left[tile] = left.T
-                pair_weight[tile] = weights
-            return carry
-
-        lax.fori_loop(0, TILES // SOME, features, 0)
-
-    def pair_forces(first, last):
-        def forces(turn, carry):
-            tiles = [turn * SOME + spot for spot in range(SOME)]
-            forms = [
-                jnp.dot(pair_left[tile], pair_right[tile], preferred_element_type=F32)
-                for tile in tiles
-            ]
-            strengths = []
-            for form in forms:
+    def pair_forces(step, halfway=None):
+        row = lax.broadcasted_iota(jnp.int32, (8, 128), 0)
+        ready, formed = {}, {}
+        for turn in range(TILES + 2 * SOON):
+            if halfway is not None and turn == TILES // 2 + SOON:
+                halfway()
+            if turn < TILES:
+                left, weights = pair_other(
+                    pool[step][other_ids[turn]], own[home_ids[turn]], row
+                )
+                ready[turn] = (left.T, weights)
+            tile = turn - SOON
+            if 0 <= tile < TILES:
+                formed[tile] = jnp.dot(
+                    ready[tile][0], pair_right[tile], preferred_element_type=F32
+                )
+            tile = turn - 2 * SOON
+            if tile >= 0:
+                form = formed.pop(tile)
                 square = jnp.maximum(form[:, 0:128], SOFTENING)
                 speed, reach = form[:, 128:256], form[:, 256:384]
                 scaled = square * reach
                 ratio = lax.rsqrt(scaled * reach)
                 overlap = jnp.maximum(reach - scaled * ratio, 0.0)
-                strengths.append(overlap * ratio * (STIFFNESS + speed * (reach * ratio)))
-            for tile, strength in zip(tiles, strengths):
-                pair_out[tile] = weighted(pair_weight[tile], strength)
-            return carry
-
-        lax.fori_loop(first, last, forces, 0)
+                strength = overlap * ratio * (STIFFNESS + speed * (reach * ratio))
+                pair_out[tile] = weighted(ready.pop(tile)[1], strength)
 
     def wall_homes():
         def some(turn, carry):
@@ -566,12 +561,13 @@
             wall_homes()
             prepare()
             wait_ghosts(0)
-            pair_features(0)
-            pair_forces(0, 1)
-            pass_far(0)
-            zh_copy(1).start()
-            start_tri(1)
-            pair_forces(1, 2)
+
+            def halfway():
+                pass_far(0)
+                zh_copy(1).start()
+                start_tri(1)
+
+            pair_forces(0, halfway)
             wait_tri(0)
             wall_features(0)
             wall_forces()
@@ -579,22 +575,19 @@
             wall_homes()
             pair_homes()
             pass_far(step)
-            if step == 1:
-                forward_tri(2)
-                pass_near(2)
             wait_tri(step)
             wall_features(step)
             wall_forces()
             wait_ghosts(step)
-            pair_features(step)
-            pair_forces(0, 2)
+            if step == 1:
+                zh_copy(2).start()
+                start_tri(2)
+            pair_forces(step)
         integrate()
         send_migrants(step)
-        if step == 0:
-            pass_near(1)
-            forward_tri(1)
-            zh_copy(2).start()
-            start_tri(2)
+        if step < 2:
+            pass_near(step + 1)
+            forward_tri(step + 1)
         take_migrants(step)
 
     pos_o[...] = bodies[0:3]
@@ -654,8 +647,6 @@
             pltpu.VMEM((TILES, 8, 128), F32),
             pltpu.VMEM((TTILES, 8, 128), F32),
             pltpu.VMEM((TILES, 64, 384), BF16),
-            pltpu.VMEM((TILES, 128, 64), BF16),
-            pltpu.VMEM((TILES, 8, 128), BF16),
             pltpu.VMEM((TTILES, 64, 256), BF16),
             pltpu.VMEM((TTILES, 128, 64), BF16),
             pltpu.VMEM((TTILES, 8, 128), BF16),

time: 70 us -> 67 us (0.957)
  Pallas kernels: 67.3 us -> 64.3 us
    pallas_call x1, Pallas kernels: 67.3 us -> 64.3 us  [shards(): pl.pallas_call(kernel, out_shape=(pltpu.VMEM((3, NBLK, 128), F32), pltpu....]
where the time goes in v3:
time: 67 us; the launch traced here: 66.8 us
  Pallas kernels  64.3 us (96%)
  local copies, waits for them, and re-layouts  1.85 us (3%)
    pallas_call x1, Pallas kernels, shards(): pl.pallas_call(kernel, out_shape=(pltpu.VMEM((3, NBLK, 128), F32), pltpu....  64.3 us
    unnamed x3, local copies, waits for them, and re-layouts  1.85 us

profile of v3, /device:TPU:1, one launch (start us, length us, event | category | flops | bytes accessed | tf_op | source)
XLA Modules:
  0.0 66.8 jit_solution(1640144010038521514)
XLA Ops:
  0.6 64.3 %shard_map.148 = (f32[3,32,128]{2,1,0:T(8,128)S(1)}, f32[3,32,128]{2,1,0:T(8,128)S(1)}, f32[32,128]{1,0:T(8,128)S(1)}) custom-call(f32[3,32,128]{2,1,0:T(8,128)} %bitcast.20, f32[3,32,128]{2,1,0:T(8,128)} %bitcast.21, f32[32,128]{1,0:T(8,128)} %bitcast.23, f32[9,16,128]{2,1,0:T(8,128)} %bitcast.18, f32[9,16,128]{2,1,0:T(8,128)} %bitcast.19, ...), custom_call_target="tpu_custom_call" | custom-call | tf_op jit(solution)/shard_map/pallas_call | solution.py:623
  65.0 0.6 copy.23
  65.6 0.6 copy.24
  66.2 0.6 copy.25

commit v4 on v3

--- a/solution.py
+++ b/solution.py
@@ -23,6 +23,10 @@
 MC = 16
 SOME = 32
 SOON = 8
+
+FAR_FIRST = [
+    4 * across + along for along in (2, 1, 3, 0) for across in (1, 3, 2, 0) if along or across
+]
 
 STIFFNESS = 20.0
 DAMPING = 2.0
@@ -218,17 +222,15 @@
 
     barrier = pltpu.get_barrier_semaphore()
 
-    def greet(hop, carry):
-        pl.semaphore_signal(barrier, inc=1, device_id=peer_of(hop)[1], device_id_type=MESH)
-        return carry
-
-    lax.fori_loop(1, GROUP, greet, 0)
-    for other in (twin, zmate, x_mate(1, zh), x_mate(2, zh), x_mate(3, zh)):
-        pl.semaphore_signal(barrier, inc=1, device_id=(other, gy, gz), device_id_type=MESH)
     for _, borrower, target in faces[:2]:
         @pl.when(borrower)
         def _():
             pl.semaphore_signal(barrier, inc=1, device_id=target, device_id_type=MESH)
+    pl.semaphore_signal(barrier, inc=1, device_id=(zmate, gy, gz), device_id_type=MESH)
+    for hop in FAR_FIRST:
+        pl.semaphore_signal(barrier, inc=1, device_id=peer_of(hop)[1], device_id_type=MESH)
+    for other in (x_mate(2, zh), x_mate(1, zh), x_mate(3, zh), twin):
+        pl.semaphore_signal(barrier, inc=1, device_id=(other, gy, gz), device_id_type=MESH)
 
     def ghost_copy(step, face, target):
         return pltpu.make_async_remote_copy(
@@ -458,20 +460,22 @@
         lax.fori_loop(0, TTILES // SOME, forces, 0)
 
     def integrate():
-        def home_sum(select, out, row):
-            high, low = split2(out[:, row, :] + out[:, row + 4, :])
-            return jnp.dot(select, high, preferred_element_type=F32) + jnp.dot(
-                select, low, preferred_element_type=F32
-            )
-
-        pairs, walls = pair_sel[...], wall_sel[...]
-        weight = home_sum(pairs, pair_out, 3)
+        def home_sums(select, out, rows):
+            terms = [out[:, row, :] + out[:, row + 4, :] for row in range(rows)]
+            parts = jnp.concatenate(split2(jnp.concatenate(terms, axis=1)), axis=0)
+            both = jnp.concatenate([select, select], axis=1)
+            sums = jnp.dot(both, parts, preferred_element_type=F32)
+            return [sums[:, 128 * row : 128 * row + 128] for row in range(rows)]
+
+        pairs = home_sums(pair_sel[...], pair_out, 4)
+        walls = home_sums(wall_sel[...], wall_out, 3)
+        weight = pairs[3]
         radius = bodies[6]
         inertia = 1.0 / (radius * radius)
         for i in range(3):
             place = bodies[i]
-            contact = (place - place[:, 0:1]) * weight - home_sum(pairs, pair_out, i)
-            pull = (contact + WALL_STIFF * home_sum(walls, wall_out, i)) * inertia
+            contact = (place - place[:, 0:1]) * weight - pairs[i]
+            pull = (contact + WALL_STIFF * walls[i]) * inertia
             if i == 2:
                 pull = pull - GRAVITY
             velocity = bodies[3 + i] + TIME_STEP * pull
@@ -480,10 +484,9 @@
 
     def send_migrants(step):
         hot = lane_hot[step]
-        parts = split3(bodies[...].reshape(7 * NBLK, 128))
-        picked = jnp.dot(parts[0], hot, preferred_element_type=F32)
-        picked = picked + jnp.dot(parts[1], hot, preferred_element_type=F32)
-        picked = picked + jnp.dot(parts[2], hot, preferred_element_type=F32)
+        parts = stacked(split3(bodies[...].reshape(7 * NBLK, 128)))
+        picked = jnp.dot(parts, hot, preferred_element_type=F32)
+        picked = (picked[0:224] + picked[224:448]) + picked[448:672]
         hit = block_hot[step, 0] > 0.5
         for row in range(7):
             line = jnp.where(hit, picked[NBLK * row : NBLK * row + NBLK], 0.0)
@@ -493,10 +496,8 @@
         for half in range(2):
             outgoing[step, half, 7:8, :] = jnp.zeros((1, 128), F32)
 
-        for along in (2, 1, 3, 0):
-            for across in (1, 3, 2, 0):
-                if along or across:
-                    mig_copy(step, 4 * across + along).start()
+        for hop in FAR_FIRST:
+            mig_copy(step, hop).start()
 
     def take_migrants(step):
         def wait(hop, carry):
@@ -522,12 +523,10 @@
         )
         dims = (((1,), (1,)), ((), ()))
         hot = lane_hot[step]
-        landed = jnp.zeros((7 * NBLK, 128), F32)
-        for part in split3(spread):
-            landed = landed + lax.dot_general(part, hot, dims, preferred_element_type=F32)
-        hits = lax.dot_general(
-            block_hot[step, 1].astype(BF16), hot, dims, preferred_element_type=F32
-        )
+        parts = stacked([*split3(spread), block_hot[step, 1].astype(BF16)])
+        landed = lax.dot_general(parts, hot, dims, preferred_element_type=F32)
+        hits = landed[672:704]
+        landed = (landed[0:224] + landed[224:448]) + landed[448:672]
         for row in range(7):
             bodies[row] = jnp.where(hits > 0.5, landed[NBLK * row : NBLK * row + NBLK], bodies[row])
 

time: 67 us -> 65.6 us (0.979)
  Pallas kernels: 64.3 us -> 63 us
    pallas_call x1, Pallas kernels: 64.3 us -> 63 us  [shards(): pl.pallas_call(kernel, out_shape=(pltpu.VMEM((3, NBLK, 128), F32), pltpu....]
where the time goes in v4:
time: 65.6 us; the launch traced here: 65.5 us
  Pallas kernels  63 us (96%)
  local copies, waits for them, and re-layouts  1.85 us (3%)
    pallas_call x1, Pallas kernels, shards(): pl.pallas_call(kernel, out_shape=(pltpu.VMEM((3, NBLK, 128), F32), pltpu....  63 us
    unnamed x3, local copies, waits for them, and re-layouts  1.85 us

profile of v4, /device:TPU:1, one launch (start us, length us, event | category | flops | bytes accessed | tf_op | source)
XLA Modules:
  0.0 65.5 jit_solution(9755798994802306844)
XLA Ops:
  0.6 63.0 %shard_map.148 = (f32[3,32,128]{2,1,0:T(8,128)S(1)}, f32[3,32,128]{2,1,0:T(8,128)S(1)}, f32[32,128]{1,0:T(8,128)S(1)}) custom-call(f32[3,32,128]{2,1,0:T(8,128)} %bitcast.20, f32[3,32,128]{2,1,0:T(8,128)} %bitcast.21, f32[32,128]{1,0:T(8,128)} %bitcast.23, f32[9,16,128]{2,1,0:T(8,128)} %bitcast.18, f32[9,16,128]{2,1,0:T(8,128)} %bitcast.19, ...), custom_call_target="tpu_custom_call" | custom-call | tf_op jit(solution)/shard_map/pallas_call | solution.py:622
  63.6 0.6 copy.23
  64.3 0.6 copy.24
  64.9 0.6 copy.25

commit v5 on v4

--- a/solution.py
+++ b/solution.py
@@ -18,6 +18,7 @@
 TILES = 64
 TTILES = 32
 TRIBLK = 16
+HALF = 8
 SLABS = 16
 GROUP = 16
 MC = 16
@@ -242,8 +243,8 @@
             device_id_type=MESH,
         )
 
-    def tri_copy(step, owner, target, send, recv):
-        part = tri[step].at[pl.ds(owner * TRIBLK, TRIBLK)]
+    def tri_copy(step, owner, target, send, recv, first=0, count=TRIBLK):
+        part = tri[step].at[pl.ds(owner * TRIBLK + first, count)]
         return pltpu.make_async_remote_copy(
             src_ref=part,
             dst_ref=part,
@@ -253,8 +254,14 @@
             device_id_type=MESH,
         )
 
-    def zh_copy(step):
-        return tri_copy(step, gx, zmate, zh_send.at[step], zh_recv.at[step])
+    def zh_copy(step, half):
+        return tri_copy(
+            step, gx, zmate, zh_send.at[step, half], zh_recv.at[step, half], HALF * half, HALF
+        )
+
+    def start_zh(step):
+        for half in range(2):
+            zh_copy(step, half).start()
 
     def core_copy(step, owner, slot):
         return tri_copy(step, owner, twin, core_send.at[step, slot], core_recv.at[step, slot])
@@ -262,8 +269,12 @@
     def x_copy(step, hop):
         return tri_copy(step, gx, x_mate(hop, zh), x_send.at[step, hop - 1], x_recv.at[step, hop - 1])
 
-    def xz_copy(step, hop):
-        return tri_copy(step, zmate, x_mate(hop, zh), xz_send.at[step, hop - 1], xz_recv.at[step, hop - 1])
+    def xz_copy(step, hop, half):
+        slot = 2 * (hop - 1) + half
+        return tri_copy(
+            step, zmate, x_mate(hop, zh), xz_send.at[step, slot], xz_recv.at[step, slot],
+            HALF * half, HALF,
+        )
 
     def mig_copy(step, hop):
         peer, target = peer_of(hop)
@@ -342,9 +353,10 @@
             x_copy(step, hop).start()
 
     def forward_tri(step):
-        zh_copy(step).wait_recv()
-        for hop in (1, 2, 3):
-            xz_copy(step, hop).start()
+        for half in range(2):
+            zh_copy(step, half).wait_recv()
+            for hop in (2, 1, 3):
+                xz_copy(step, hop, half).start()
         core_copy(step, zmate, 1).start()
 
     def pass_near(step):
@@ -353,8 +365,9 @@
             core_copy(step, x_mate(4 - hop, zh), 1 + hop).start()
 
     def pass_far(step):
-        for hop in (1, 2, 3):
-            xz_copy(step, hop).wait_recv()
+        for hop in (1, 3, 2):
+            for half in range(2):
+                xz_copy(step, hop, half).wait_recv()
             core_copy(step, x_mate(4 - hop, 1 - zh), 4 + hop).start()
 
     def wait_tri(step):
@@ -546,7 +559,7 @@
 
     for step in range(STEPS):
         if step == 0:
-            zh_copy(0).start()
+            start_zh(0)
         else:
             lend(step)
         send_ghosts(step)
@@ -563,7 +576,7 @@
 
             def halfway():
                 pass_far(0)
-                zh_copy(1).start()
+                start_zh(1)
                 start_tri(1)
 
             pair_forces(0, halfway)
@@ -579,7 +592,7 @@
             wall_forces()
             wait_ghosts(step)
             if step == 1:
-                zh_copy(2).start()
+                start_zh(2)
                 start_tri(2)
             pair_forces(step)
         integrate()
@@ -597,10 +610,12 @@
             @pl.when(borrower)
             def _():
                 ghost_copy(step, face, target).wait_send()
-        zh_copy(step).wait_send()
+        for half in range(2):
+            zh_copy(step, half).wait_send()
+            for hop in (1, 2, 3):
+                xz_copy(step, hop, half).wait_send()
         for hop in (1, 2, 3):
             x_copy(step, hop).wait_send()
-            xz_copy(step, hop).wait_send()
         for slot in range(8):
             core_copy(step, gx, slot).wait_send()
 
@@ -654,12 +669,12 @@
             dma((STEPS, 6)),
             dma((STEPS, GROUP)),
             dma((STEPS, GROUP)),
-            dma((STEPS,)),
-            dma((STEPS,)),
+            dma((STEPS, 2)),
+            dma((STEPS, 2)),
             dma((STEPS, 3)),
             dma((STEPS, 3)),
-            dma((STEPS, 3)),
-            dma((STEPS, 3)),
+            dma((STEPS, 6)),
+            dma((STEPS, 6)),
             dma((STEPS, 8)),
             dma((STEPS, 8)),
         ],

time: 65.6 us -> 65.9 us (level)
  no operation moved by 1% of the time
where the time goes in v5:
time: 65.9 us; the launch traced here: 65.5 us
  Pallas kernels  63 us (96%)
  local copies, waits for them, and re-layouts  1.85 us (3%)
    pallas_call x1, Pallas kernels, shards(): pl.pallas_call(kernel, out_shape=(pltpu.VMEM((3, NBLK, 128), F32), pltpu....  63 us
    unnamed x3, local copies, waits for them, and re-layouts  1.85 us

profile of v5, /device:TPU:1, one launch (start us, length us, event | category | flops | bytes accessed | tf_op | source)
XLA Modules:
  0.0 65.5 jit_solution(12765537192081955849)
XLA Ops:
  0.6 63.0 %shard_map.148 = (f32[3,32,128]{2,1,0:T(8,128)S(1)}, f32[3,32,128]{2,1,0:T(8,128)S(1)}, f32[32,128]{1,0:T(8,128)S(1)}) custom-call(f32[3,32,128]{2,1,0:T(8,128)} %bitcast.20, f32[3,32,128]{2,1,0:T(8,128)} %bitcast.21, f32[32,128]{1,0:T(8,128)} %bitcast.23, f32[9,16,128]{2,1,0:T(8,128)} %bitcast.18, f32[9,16,128]{2,1,0:T(8,128)} %bitcast.19, ...), custom_call_target="tpu_custom_call" | custom-call | tf_op jit(solution)/shard_map/pallas_call | solution.py:637
  63.6 0.6 copy.23
  64.2 0.6 copy.24
  64.9 0.6 copy.25
